TPU v7x, 128 devices: a whole 4x4x4 slice. The times are simulated.
128 devices in a mesh: fsdp: 32 (over z_lo, x, y), dp: 4 (over z_hi, core).
Axes of the slice: x: 4, y: 4, z: 4 (z_hi: 2, z_lo: 2; z = z_hi * 2 + z_lo), core: 2. Of those that a mesh axis runs over, the one named last changes fastest.
Arguments:
- acts: bfloat16 [65536, 8192], P(('fsdp', 'dp')), may hold values from -60 to 60
- cotangent: bfloat16 [65536, 1024], P(('fsdp', 'dp')), may hold values from -6 to 6
- master: float32 [8192, 1024], P(('fsdp', 'dp')), may hold values from -0.12 to 0.12
- moment1: float32 [8192, 1024], P(('fsdp', 'dp')), may hold values from -0.000103580095 to 0.000103580095
- moment2: float32 [8192, 1024], P(('fsdp', 'dp')), may hold values from 1.1920929e-09 to 1.1920929e-08
- hidden_in: bfloat16 [4, 4, 32, 32, 1024], P(None, 'dp', 'fsdp'), may hold values from -6 to 6
- k_cache: bfloat16 [4, 32, 32, 512, 128], P('dp', 'fsdp'), may hold values from -8 to 8
- v_cache: bfloat16 [4, 32, 32, 512, 128], P('dp', 'fsdp'), may hold values from -6 to 6
- k_new: bfloat16 [4, 4, 32, 32, 128], P(None, 'dp', 'fsdp'), may hold values from -15 to 15
- queries: bfloat16 [4, 4, 32, 32, 1024], P(None, 'dp', 'fsdp'), may hold values from -200 to 200
- cache_len: int32 [4, 4, 32], P('dp'), may hold values from 64 to 508, as said below
Outputs:
- new_master: float32 [8192, 1024], P(('fsdp', 'dp'))
- attn_out: bfloat16 [4, 4, 32, 32, 1024], P(None, 'dp', 'fsdp')
Inputs may be any that keep to these rules, and one draw needn't show every extreme that they name: `cache_len`: every sequence has between 64 and 508 filled slots; the first sequence of each replica has exactly 508.
All inputs are finite; a program needn't handle non-finite values.
Results may differ from a plain program's by a relative error of at most 0.0055.
Values may be sent and summed in bfloat16 or wider, within the bound.
A program may use at most 128 MiB of HBM per device.

v0:
```python
import jax
import jax.numpy as jnp
from jax import lax
from jax.sharding import PartitionSpec as P


def partner_2(value, axis, bit):
    mask = 2**bit
    pairs = [(source, source ^ mask) for source in range(lax.axis_size(axis))]
    return lax.ppermute(value, axis, pairs)


def attend(query, keys, values, knew, vnew, lens):
    steps, rows = (query.shape[0], query.shape[1])
    hsize = keys.shape[-1]
    qh = query.reshape(steps, rows, -1, hsize)
    scale = hsize ** (-0.5)
    sc = jnp.einsum("srhd,rcd->srhc", qh, keys, preferred_element_type=jnp.float32) * scale
    sn = jnp.einsum("srhd,trd->srht", qh, knew, preferred_element_type=jnp.float32) * scale
    cmask = jnp.arange(keys.shape[1])[None, :] < lens[:, None]
    nmask = jnp.arange(steps)[None, :] <= jnp.arange(steps)[:, None]
    sc = jnp.where(cmask[None, :, None, :], sc, -1e30)
    sn = jnp.where(nmask[:, None, None, :], sn, -1e30)
    top = jnp.maximum(jnp.max(sc, -1), jnp.max(sn, -1))
    ec = jnp.exp(sc - top[..., None])
    en = jnp.exp(sn - top[..., None])
    den = jnp.sum(ec, -1) + jnp.sum(en, -1)
    out = jnp.einsum(
        "srhc,rcd->srhd", ec.astype(jnp.bfloat16), values, preferred_element_type=jnp.float32
    )
    out = out + jnp.einsum(
        "srht,trd->srhd", en.astype(jnp.bfloat16), vnew, preferred_element_type=jnp.float32
    )
    return (out / den[..., None]).reshape(steps, rows, -1).astype(jnp.bfloat16)


def on_device(
    acts,
    cotangent,
    master,
    moment1,
    moment2,
    hidden_in,
    k_cache,
    v_cache,
    k_new,
    queries,
    cache_len,
):
    hsize = k_cache.shape[-1]
    heads_kv = master.shape[1] // hsize
    grad = lax.psum_scatter(
        lax.dot_general(
            acts, cotangent, (((0,), (0,)), ((), ())), preferred_element_type=jnp.float32
        ),
        ("fsdp", "dp"),
        scatter_dimension=0,
        tiled=True,
    )
    total = lax.psum(jnp.sum(grad * grad), ("fsdp", "dp"))
    clipped = grad * jnp.minimum(1.0, 1.0 / (jnp.sqrt(total) + 1e-06))
    mom = 0.9 * moment1 + 0.1 * clipped
    sec = 0.95 * moment2 + 0.05 * clipped * clipped
    update = mom / (1.0 - 0.9**10) / (jnp.sqrt(sec / (1.0 - 0.95**10)) + 1e-08)
    new_master = master - 0.1 * (update + 0.1 * master)
    shard_bf = new_master.astype(jnp.bfloat16)
    position = lax.axis_index("fsdp")
    head = position % heads_kv
    replica = position // heads_kv
    whole = lax.all_gather(shard_bf, ("fsdp", "dp"), axis=0, tiled=True)
    w_head = lax.dynamic_slice_in_dim(whole, head * hsize, hsize, 1)
    gathered = hidden_in[:, 0, 0]
    for bit in range(heads_kv.bit_length() - 1):
        partner = partner_2(gathered, "fsdp", bit)
        upper = position // (1 << bit) % 2 == 1
        first = jnp.where(upper, partner, gathered)
        second = jnp.where(upper, gathered, partner)
        gathered = jnp.concatenate([first, second], -1)
    steps, rows, width = gathered.shape
    vnew = jnp.dot(gathered.reshape(-1, width), w_head, preferred_element_type=jnp.float32) * (
        32.0 * width ** (-0.5)
    )
    vnew = vnew.astype(jnp.bfloat16).reshape(steps, rows, hsize)
    lens = lax.dynamic_index_in_dim(cache_len[0], replica, 0, keepdims=False)
    result = attend(queries[:, 0, 0], k_cache[0, 0], v_cache[0, 0], k_new[:, 0, 0], vnew, lens)
    return (new_master, result.reshape(steps, 1, 1, rows, -1))


def solution(mesh):
    in_specs = (
        P(("fsdp", "dp"), None),
        P(("fsdp", "dp"), None),
        P(("fsdp", "dp"), None),
        P(("fsdp", "dp"), None),
        P(("fsdp", "dp"), None),
        P(None, "dp", "fsdp", None, None),
        P("dp", "fsdp", None, None, None),
        P("dp", "fsdp", None, None, None),
        P(None, "dp", "fsdp", None, None),
        P(None, "dp", "fsdp", None, None),
        P("dp", None, None),
    )
    out_specs = (P(("fsdp", "dp"), None), P(None, "dp", "fsdp", None, None))
    return jax.shard_map(
        on_device, mesh=mesh, in_specs=in_specs, out_specs=out_specs, check_vma=False
    )
```

profile of v0, /device:TPU:1, one launch (start us, length us, event | category | flops | bytes accessed | tf_op | source)
XLA Modules:
  0.0 1051.1 jit_solution(11226398811800416049)
XLA Ops:
  7.2 0.0 copy-start
  7.2 0.0 reduce-scatter.2.cloned.1.call-start
  7.2 1.2 copy-done
  8.4 18.7 %fusion.47 = f32[8192,1024]{1,0:T(8,128)} fusion(bf16[512,8192]{1,0:T(8,128)(2,1)} %param.11, bf16[512,1024]{1,0:T(8,128)(2,1)S(1)} %copy-done), kind=kOutput, calls=%fused_computation.60 | convolution fusion | flops 8589934592 | bytes 42991616 | tf_op jit(solution)/shard_map/dot_general | solution.py:53
  27.1 0.0 copy-start.9
  27.1 0.0 copy-start.10
  27.1 0.0 copy-start.11
  27.1 0.0 copy-start.12
  27.1 0.0 reduce-scatter.2.cloned.1.call-update
  27.2 0.0 copy-start.8
  27.2 0.0 all-gather.2.cloned.1.call-start
  27.2 718.2 %reduce-scatter.2.cloned.1.call-done = f32[64,1024]{1,0:T(8,128)} async-done(((f32[8192,1024]{1,0:T(8,128)}), f32[64,1024]{1,0:T(8,128)}) %reduce-scatter.2.cloned.1.call-update) | async-done | bytes 262160 | tf_op jit(solution)/shard_map/reduce_scatter | solution.py:52
  745.4 1.6 multiply_reduce_fusion
  747.1 68.5 %psum.7 = f32[]{:T(128)} all-reduce(f32[]{:T(128)} %multiply_reduce_fusion), channel_id=1, replica_groups=mesh['fsdp'=32,'dp'=4] {'fsdp','dp'}, use_global_device_ids=true, to_apply=%region_2.0 | all-reduce | flops 1 | bytes 8 | tf_op jit(solution)/shard_map/psum | solution.py:60
  816.3 0.0 copy-done.9
  816.3 0.0 copy-done.10
  816.3 0.0 copy-done.11
  816.3 1.9 fusion.45
  818.2 0.0 all-gather.2.cloned.1.call-update
  818.2 0.0 copy-done.12
  818.3 0.1 collective-permute-start
  818.4 0.7 dynamic-slice_bitcast_fusion
  819.1 6.0 collective-permute-done
  825.1 0.0 copy-start.2
  825.1 2.1 collective-permute-start.1
  827.2 0.1 iota_compare_fusion
  827.4 0.0 copy-done.8
  827.4 0.0 copy-start.3
  827.5 3.8 bitcast_reduce_fusion
  831.3 0.0 copy-done.2
  831.3 0.0 copy-done.3
  831.3 0.0 copy-start.13
  831.3 9.6 collective-permute-done.1
  840.9 0.0 copy-start.4
  840.9 1.4 broadcast_select_fusion.3
  842.3 1.1 pad_maximum_fusion.1
  843.4 0.0 collective-permute-start.2
  843.4 0.0 copy-done.13
  843.4 0.0 copy-done.4
  843.4 1.3 fusion.46
  844.7 0.0 copy-start.6
  844.7 0.3 fusion.36
  845.0 0.4 copy-done.6
  845.4 0.8 fusion.7
  846.2 3.9 fusion.10
  850.2 25.2 %collective-permute-done.2 = bf16[4,32,4096]{2,1,0:T(8,128)(2,1)} collective-permute-done((bf16[4,32,4096]{2,1,0:T(8,128)(2,1)}, bf16[4,32,4096]{2,1,0:T(8,128)(2,1)}, u32[]{:S(2)}, u32[]{:S(2)}) %collective-permute-start.2) | collective-permute-done | bytes 1048608 | tf_op jit(solution)/shard_map/ppermute | solution.py:10
  875.3 1.8 broadcast_select_fusion.1
  877.2 0.1 pad_maximum_fusion
  877.3 163.2 %all-gather.2.cloned.1.call-done = bf16[8192,1024]{1,0:T(8,128)(2,1)} async-done(((bf16[64,1024]{1,0:T(8,128)(2,1)}), bf16[8192,1024]{1,0:T(8,128)(2,1)}) %all-gather.2.cloned.1.call-update) | async-done | bytes 16777232 | tf_op jit(solution)/shard_map/all_gather | solution.py:70
  1040.5 0.0 copy-start.5
  1040.5 0.0 copy-start.7
  1040.5 0.0 copy-start.1
  1040.5 2.4 fusion.20
  1043.0 0.0 copy-done.5
  1043.0 0.0 copy-done.7
  1043.0 0.4 fusion.14
  1043.4 0.1 convert_element_type.30
  1043.4 0.8 copy.17
  1044.2 0.0 copy-done.1
  (6 shorter events, 0.2 us)
Async XLA Ops:
  7.2 1.2 copy-start
  7.2 738.3 %reduce-scatter.2.cloned.1.call-start = ((), (), s32[]{:S(2)}) async-start(), calls=%async_computation.1 | async-start | bytes 33816576 | tf_op jit(solution)/shard_map/reduce_scatter | solution.py:52
  27.1 789.1 %copy-start.9 = (f32[64,1024]{1,0:T(8,128)S(1)}, f32[64,1024]{1,0:T(8,128)}, u32[]{:S(2)}) copy-start(f32[64,1024]{1,0:T(8,128)} %param.13) | copy-start | bytes 786436
  27.1 789.2 %copy-start.10 = (f32[64,1024]{1,0:T(8,128)S(1)}, f32[64,1024]{1,0:T(8,128)}, u32[]{:S(2)}) copy-start(f32[64,1024]{1,0:T(8,128)} %param.15) | copy-start | bytes 786436
  27.1 789.2 %copy-start.11 = (f32[64,1024]{1,0:T(8,128)S(1)}, f32[64,1024]{1,0:T(8,128)}, u32[]{:S(2)}) copy-start(f32[64,1024]{1,0:T(8,128)} %param.14) | copy-start | bytes 786436
  27.1 791.1 %copy-start.12 = (bf16[4,1,1,32,1024]{4,3,2,1,0:T(8,128)(2,1)S(1)}, bf16[4,1,1,32,1024]{4,3,2,1,0:T(8,128)(2,1)}, u32[]{:S(2)}) copy-start(bf16[4,1,1,32,1024]{4,3,2,1,0:T(8,128)(2,1)} %param.16) | copy-start | bytes 786436
  27.2 800.2 %copy-start.8 = (bf16[4,1,1,32,1024]{4,3,2,1,0:T(8,128)(2,1)S(1)}, bf16[4,1,1,32,1024]{4,3,2,1,0:T(8,128)(2,1)}, u32[]{:S(2)}) copy-start(bf16[4,1,1,32,1024]{4,3,2,1,0:T(8,128)(2,1)} %param.20) | copy-start | bytes 786436
  27.2 1013.3 %all-gather.2.cloned.1.call-start = ((), (), s32[]{:S(2)}) async-start(), calls=%async_computation.2 | async-start | bytes 16908288 | tf_op jit(solution)/shard_map/all_gather | solution.py:70
  818.3 6.8 collective-permute-start
  825.1 6.2 copy-start.2
  825.1 15.8 %collective-permute-start.1 = (bf16[4,32,2048]{2,1,0:T(8,128)(2,1)S(1)}, bf16[4,32,2048]{2,1,0:T(8,128)(2,1)}, u32[]{:S(2)}, u32[]{:S(2)}) collective-permute-start(bf16[4,32,2048]{2,1,0:T(8,128)(2,1)S(1)} %pad_maximum_fusion.2), channel_id=1, source_target_pairs={{0,8},{4,12},{8,0},{12,4},{16,24},{20,28},{24,16},{28,20},{32,40},... | collective-permute-start | bytes 1572872 | tf_op jit(solution)/shard_map/ppermute | solution.py:10
  827.4 3.9 copy-start.3
  831.3 12.1 %copy-start.13 = (bf16[4,1,1,32,128]{4,3,2,1,0:T(8,128)(2,1)S(1)}, bf16[4,1,1,32,128]{4,3,2,1,0:T(8,128)(2,1)}, u32[]{:S(2)}) copy-start(bf16[4,1,1,32,128]{4,3,2,1,0:T(8,128)(2,1)} %param.19) | copy-start | bytes 98308
  840.9 2.5 copy-start.4
  843.4 32.0 %collective-permute-start.2 = (bf16[4,32,4096]{2,1,0:T(8,128)(2,1)}, bf16[4,32,4096]{2,1,0:T(8,128)(2,1)}, u32[]{:S(2)}, u32[]{:S(2)}) collective-permute-start(bf16[4,32,4096]{2,1,0:T(8,128)(2,1)} %pad_maximum_fusion.1), channel_id=1, source_target_pairs={{0,16},{4,20},{8,24},{12,28},{16,0},{20,4},{24,8},{28,12},{32,48},... | collective-permute-start | bytes 3145736 | tf_op jit(solution)/shard_map/ppermute | solution.py:10
  844.7 0.7 copy-start.6
  1040.5 2.4 copy-start.5
  1040.5 2.4 copy-start.7
  1040.5 3.7 copy-start.1
Sparse Core Ops, SparseCore 0:
  27.3 718.0 reduce-scatter.1
  818.4 222.1 all-gather.1
where the time goes:
time: 1050 us
  waiting for transfers between devices  922 us (88%)
  blocking collectives  68.5 us (7%)
  matrix products  30.6 us (3%)
  between operations  15.1 us (1%)
    reduce_scatter x1, waiting for transfers between devices, on_device(): lax.psum_scatter(lax.dot_general(acts, cotangent, (((0,), (0,)), ((), ())...  718 us
    all_gather x1, waiting for transfers between devices, on_device(): whole = lax.all_gather(shard_bf, ('fsdp', 'dp'), axis=0, tiled=True)  163 us
    psum x1, blocking collectives, on_device(): total = lax.psum(jnp.sum(grad * grad), ('fsdp', 'dp'))  68.5 us
    ppermute x3, waiting for transfers between devices, partner_2(): return lax.ppermute(value, axis, pairs)  40.7 us
  transfers between devices with their start and end apart: 5, of which 5 were waited for; matrix products, arithmetic and copies ran while one was open for 1% of the time, Pallas kernels for 0%

commit v1 on v0

v1 whole, which is shorter than its diff:
```python
import functools

import jax
import jax.numpy as jnp
from jax import lax
from jax.experimental import pallas as pl
from jax.experimental.pallas import tpu as pltpu
from jax.sharding import PartitionSpec as P

MESH = pl.DeviceIdType.MESH
F32 = jnp.float32
BF16 = jnp.bfloat16
PARTS = ((0, 176), (176, 176), (352, 160))
NT = (((1,), (1,)), ((), ()))


def coordinates():
    f, d = lax.axis_index("fsdp"), lax.axis_index("dp")
    return ((f // 4) % 4, f % 4, (d // 2) * 2 + f // 16), d % 2


def device(pos, core):
    x, y, z = pos
    return ((z % 2) * 16 + x * 4 + y, (z // 2) * 2 + core)


def shifted(pos, dim, delta):
    return tuple((v + delta) % 4 if i == dim else v for i, v in enumerate(pos))


def kernel(
    lens, acts, cot, master, mom1, mom2, hid, keys, vals, knew, query,
    nm_out, at_out,
    abuf, cbuf, ct, g0, g1, g2, ra0, ra1, ra2, s0, s1, s2, rb0, rb1, rb2, t0, t1, t2, rc0, rc1, rc2,
    ms, gt, nsend, nrecv, nmx, nmr, wsend, wbuf, vf, vs, vr,
    kbuf, vbuf, qbuf, knbuf, hbuf, qs, kns, acc, ens, accn, enn,
    loc, asend, arecv, xsend, xrecv, p1s, p1r, p2s, p2r, p3s, p3r, nss, nsr, ws, wr, fs, fr, vss, vsr, osend, orecv,
):
    pos, core = coordinates()
    x, y, z = pos
    other = 1 - core
    me = device(pos, core)
    sib = device(pos, other)
    gs, ras, ss, rbs, ts, rcs = (g0, g1, g2), (ra0, ra1, ra2), (s0, s1, s2), (rb0, rb1, rb2), (t0, t1, t2), (rc0, rc1, rc2)

    def copy(src, dst, sem):
        return pltpu.make_async_copy(src, dst, sem)

    def remote(src, dst, ssem, rsem, dev):
        return pltpu.make_async_remote_copy(
            src_ref=src, dst_ref=dst, send_sem=ssem, recv_sem=rsem, device_id=dev, device_id_type=MESH
        )

    def drain(ref, sem):
        pltpu.make_async_copy(ref, ref, sem).wait()

    def lanes(k, j):
        xb, yb = j // 4, j % 4
        zb = (k + 8 - xb - yb) % 4
        return pl.ds(pl.multiple_of((((zb % 2) * 16 + xb * 4 + yb) * 2 + zb // 2) * 128, 128), 128)

    half = pl.ds(pl.multiple_of(core * 512, 512), 512)
    far = pl.ds(pl.multiple_of(other * 512, 512), 512)
    mine = pl.ds(pl.multiple_of(core * 64, 64), 64)
    theirs = pl.ds(pl.multiple_of(other * 64, 64), 64)

    barrier = pltpu.get_barrier_semaphore()
    pl.semaphore_signal(barrier, inc=1, device_id=sib, device_id_type=MESH)
    for dim in range(3):
        for delta in (1, 2, 3):
            pl.semaphore_signal(barrier, inc=1, device_id=device(shifted(pos, dim, delta), core), device_id_type=MESH)

    copy(cot.at[:, half], cbuf.at[0], loc.at[4]).start()
    for k in range(4):
        @pl.loop(0, 16)
        def _(j):
            to = pl.ds(pl.multiple_of(j * 128, 128), 128)
            copy(acts.at[:, lanes(k, j)], abuf.at[k, pl.ds(0, 512), to], loc.at[k]).start()
    copy(query, qbuf, loc.at[6]).start()
    copy(knew, knbuf, loc.at[7]).start()
    copy(keys, kbuf, loc.at[8]).start()
    copy(vals, vbuf, loc.at[9]).start()
    for i, ref in enumerate((master, mom1, mom2)):
        copy(ref.at[:, half], ms.at[i, mine], loc.at[10 + i]).start()
    copy(hid, hbuf, loc.at[5]).start()

    pl.semaphore_wait(barrier, 10)

    remote(cot.at[:, far], cbuf.at[1], xsend.at[0], xrecv.at[0], sib).start()
    for k in range(4):
        @pl.loop(0, 16)
        def _(j):
            to = pl.ds(pl.multiple_of(j * 128, 128), 128)
            remote(acts.at[:, lanes(k, j)], abuf.at[k, pl.ds(512, 512), to], asend.at[k], arecv.at[k], sib).start()
    for i, ref in enumerate((master, mom1, mom2)):
        remote(ref.at[:, far], ms.at[i, mine], xsend.at[1 + i], xrecv.at[1 + i], sib).start()

    copy(cot.at[:, half], cbuf.at[0], loc.at[4]).wait()
    ct[:, 0:512] = cbuf[0].T
    drain(cbuf.at[1], xrecv.at[0])
    ct[:, 512:1024] = cbuf[1].T

    for k in range(4):
        drain(abuf.at[k, pl.ds(0, 512)], loc.at[k])
        drain(abuf.at[k, pl.ds(512, 512)], arecv.at[k])

        @pl.loop(0, 8)
        def _(jp):
            cols = pl.ds(pl.multiple_of(jp * 256, 256), 256)
            res = jnp.dot(ct[...], abuf[k, :, cols], preferred_element_type=F32).astype(BF16)
            xb = jp // 2
            for e in range(2):
                yb = (jp % 2) * 2 + e
                zb = (k + 8 - xb - yb) % 4
                piece = res[:, e * 128 : (e + 1) * 128]
                g0[k, xb, yb] = piece[0:176]
                g1[k, yb, zb] = piece[176:352]
                g2[k, zb, xb] = piece[352:512]

        for p in range(3):
            for delta in (1, 2, 3):
                to = shifted(pos, p, delta)
                remote(
                    gs[p].at[k, to[p]], ras[p].at[k, delta - 1], p1s.at[p], p1r.at[k, p], device(to, core)
                ).start()

    copy(query, qbuf, loc.at[6]).wait()
    copy(knew, knbuf, loc.at[7]).wait()
    for s in range(4):
        for h in range(8):
            qs[pl.ds(s * 8 + h, 32, stride=32), :] = qbuf[s, :, h * 128 : (h + 1) * 128].astype(F32)
    kns[...] = jnp.zeros_like(kns)
    for s in range(4):
        kns[pl.ds(s, 32, stride=8), :] = knbuf[s].astype(F32)
    copy(keys, kbuf, loc.at[8]).wait()
    copy(vals, vbuf, loc.at[9]).wait()
    replica = (z % 2) * 2 + x // 2
    scale = 128 ** (-0.5)

    def attend(i):
        rows = pl.ds(pl.multiple_of(i * 32, 32), 32)
        qi = qs[rows, :].astype(BF16)
        sc = lax.dot_general(qi, kbuf[i], NT, preferred_element_type=F32) * scale
        slot = lax.broadcasted_iota(jnp.int32, (32, 512), 1)
        sc = jnp.where(slot < lens[replica, i], sc, -1e30)
        kn = kns[pl.ds(pl.multiple_of(i * 8, 8), 8), :].astype(BF16)
        sn = lax.dot_general(qi, kn, NT, preferred_element_type=F32) * scale
        step = lax.broadcasted_iota(jnp.int32, (32, 8), 0) // 8
        sn = jnp.where(lax.broadcasted_iota(jnp.int32, (32, 8), 1) <= step, sn, -1e30)
        top = jnp.maximum(jnp.max(sc, 1, keepdims=True), jnp.max(sn, 1, keepdims=True))
        ec = jnp.exp(sc - top)
        en = jnp.exp(sn - top)
        inv = 1.0 / (jnp.sum(ec, 1, keepdims=True) + jnp.sum(en, 1, keepdims=True))
        out = jnp.dot(ec.astype(BF16), vbuf[i], preferred_element_type=F32)
        acc[rows, :] = out * inv
        ens[rows, 0:8] = en.astype(BF16).astype(F32) * inv

    def attend_rows(first):
        @pl.loop(0, 4)
        def _(i):
            attend(first + 2 * i)
            attend(first + 2 * i + 1)

    def first_sum(k):
        for p in range(3):
            b = (p + 1) % 3
            drain(ras[p].at[k], p1r.at[k, p])

            @pl.loop(0, 4)
            def _(i):
                total = gs[p][k, pos[p], i].astype(F32)
                for slot in range(3):
                    total += ras[p][k, slot, i].astype(F32)
                ss[p][k, i] = total.astype(BF16)

            for delta in (1, 2, 3):
                to = shifted(pos, b, delta)
                remote(
                    ss[p].at[k, to[b]], rbs[p].at[k, delta - 1], p2s.at[p], p2r.at[k, p], device(to, core)
                ).start()

    def second_sum(k):
        for p in range(3):
            b, c = (p + 1) % 3, (p + 2) % 3
            drain(rbs[p].at[k], p2r.at[k, p])
            total = ss[p][k, pos[b]].astype(F32)
            for slot in range(3):
                total += rbs[p][k, slot].astype(F32)
            ts[p][k] = total.astype(BF16)
            target = (k + 8 - pos[p] - pos[b]) % 4
            delta = (target + 4 - pos[c]) % 4

            @pl.when(delta != 0)
            def _():
                remote(
                    ts[p].at[k], rcs[p].at[delta - 1], p3s.at[p], p3r.at[p], device(shifted(pos, c, delta), core)
                ).start()

    attend_rows(0)
    first_sum(0)
    attend_rows(8)
    first_sum(1)
    second_sum(0)
    attend_rows(16)
    first_sum(2)
    second_sum(1)
    attend_rows(24)
    for j in range(32):
        accn[j] = acc[pl.ds(j, 32, stride=32), :]
        enn[j] = ens[pl.ds(j, 32, stride=32), :]
    first_sum(3)
    second_sum(2)
    second_sum(3)

    own = (x + y + z) % 4
    for p, (first, size) in enumerate(PARTS):
        drain(rcs[p], p3r.at[p])
        total = ts[p][own].astype(F32)
        for slot in range(3):
            total += rcs[p][slot].astype(F32)
        gt[pl.ds(first, size), :] = total

    square = jnp.zeros((8, 128), F32)
    for i in range(64):
        part = gt[pl.ds(i * 8, 8), :]
        square += part * part
    for stage in range(4):
        nsend[stage] = square
        if stage == 0:
            remote(nsend.at[0], nrecv.at[0, 0], nss.at[0], nsr.at[0], sib).start()
            drain(nrecv.at[0, 0], nsr.at[0])
            square += nrecv[0, 0]
        else:
            for delta in (1, 2, 3):
                remote(
                    nsend.at[stage], nrecv.at[stage, delta - 1], nss.at[stage], nsr.at[stage],
                    device(shifted(pos, stage - 1, delta), core),
                ).start()
            drain(nrecv.at[stage], nsr.at[stage])
            for slot in range(3):
                square += nrecv[stage, slot]
    gnorm = jnp.sqrt(jnp.sum(square, keepdims=True))
    clip = jnp.minimum(1.0, 1.0 / (gnorm + 1e-06))

    for i in range(3):
        drain(ms.at[i, mine], loc.at[10 + i])
        drain(ms.at[i, theirs], xrecv.at[1 + i])
    for j in range(4):
        cols = slice(j * 128, (j + 1) * 128)
        clipped = gt[pl.ds(j * 128, 128), :].T * clip
        mom = 0.9 * ms[1, :, cols] + 0.1 * clipped
        sec = 0.95 * ms[2, :, cols] + 0.05 * clipped * clipped
        update = mom / (1.0 - 0.9**10) / (jnp.sqrt(sec / (1.0 - 0.95**10)) + 1e-08)
        weights = ms[0, :, cols]
        weights = weights - 0.1 * (update + 0.1 * weights)
        nmx[:, cols] = weights
        wsend[:, cols] = weights.astype(BF16)

    place = pl.ds(pl.multiple_of((y * 2 + z // 2) * 128, 128), 128)
    number = (y % 2) * 4 + (z // 2) * 2 + core
    to_core = y // 2

    def target(q):
        to = ((z % 2) + 2 * (q // 4), x, (z + q) % 4)
        same = (to[0] == x) & (to[1] == y) & (to[2] == z) & (to_core == core)
        return device(to, to_core), same

    @pl.loop(0, 8)
    def _(q):
        dev, same = target(q)

        @pl.when(jnp.logical_not(same))
        def _():
            remote(wsend, wbuf.at[place, half], ws.at[q], wr.at[number], dev).start()

        @pl.when(same)
        def _():
            copy(wsend, wbuf.at[place, half], wr.at[number]).start()

    remote(nmx.at[theirs], nmr, osend.at[0], orecv.at[0], sib).start()
    nm_out[:, half] = nmx[mine, :]
    copy(hid, hbuf, loc.at[5]).wait()

    @pl.loop(0, 8)
    def _(sl):
        rows = pl.ds(pl.multiple_of(((2 * core + sl // 4) * 2 + (sl // 2) % 2) * 128, 128), 128)
        cols = pl.ds(pl.multiple_of((sl % 2) * 512, 512), 512)
        drain(wbuf.at[rows, cols], wr.at[sl])
        remote(wbuf.at[rows, cols], wbuf.at[rows, cols], fs.at[0], fr.at[0], sib).start()

    @pl.loop(0, 4)
    def _(n):
        cols = pl.ds(pl.multiple_of(n * 256, 256), 256)
        res = jnp.dot(hbuf[:, half], wbuf[half, cols], preferred_element_type=F32)
        vf[2 * n] = res[:, 0:128]
        vf[2 * n + 1] = res[:, 128:256]

    drain(nmr, orecv.at[0])
    nm_out[:, far] = nmr[...]
    drain(wbuf.at[far], fr.at[0])
    head = (x % 2) * 4 + y

    @pl.loop(0, 4)
    def _(n):
        cols = pl.ds(pl.multiple_of(n * 256, 256), 256)
        res = jnp.dot(hbuf[:, far], wbuf[far, cols], preferred_element_type=F32)
        for e in range(2):
            to_head = 2 * n + e
            total = vf[to_head] + res[:, e * 128 : (e + 1) * 128]
            vf[to_head] = total
            vs[to_head] = total.astype(BF16)
            delta = (to_head + 8 - head) % 8
            to = ((x // 2) * 2 + to_head // 4, to_head % 4, z)

            @pl.when(delta != 0)
            def _():
                remote(vs.at[to_head], vr.at[delta - 1], vss.at[0], vsr.at[0], device(to, core)).start()

    drain(vr, vsr.at[0])
    total = vf[head]
    for slot in range(7):
        total += vr[slot].astype(F32)
    vnew = (total * (32.0 * 8192 ** (-0.5))).astype(BF16).astype(F32)
    for s in range(4):
        for h in range(8):
            out = accn[s * 8 + h]
            weight = enn[s * 8 + h]
            for t in range(s + 1):
                out += weight[:, t : t + 1] * vnew[t * 32 : (t + 1) * 32]
            at_out[s, :, h * 128 : (h + 1) * 128] = out.astype(BF16)

    drain(cbuf.at[1], xsend.at[0])
    for i in range(3):
        drain(ms.at[i, theirs], xsend.at[1 + i])
    for k in range(4):
        drain(abuf.at[k, pl.ds(512, 512)], asend.at[k])
    for p in range(3):
        drain(ras[p], p1s.at[p])
        drain(rbs[p], p2s.at[p])
        drain(rcs[p], p3s.at[p])
    drain(nrecv.at[0, 0], nss.at[0])
    for stage in range(1, 4):
        drain(nrecv.at[stage], nss.at[stage])

    @pl.loop(0, 8)
    def _(q):
        _, same = target(q)

        @pl.when(jnp.logical_not(same))
        def _():
            drain(wsend, ws.at[q])

    drain(nmr, osend.at[0])
    drain(wbuf.at[half], fs.at[0])
    drain(vr, vss.at[0])


def scratch():
    v, sem = pltpu.VMEM, pltpu.SemaphoreType.DMA
    sizes = [size for _, size in PARTS]
    return [
        v((4, 1024, 2048), BF16), v((2, 512, 512), BF16), v((512, 1024), BF16),
        *[v((4, 4, 4, n, 128), BF16) for n in sizes],
        *[v((4, 3, 4, n, 128), BF16) for n in sizes],
        *[v((4, 4, n, 128), BF16) for n in sizes],
        *[v((4, 3, n, 128), BF16) for n in sizes],
        *[v((4, n, 128), BF16) for n in sizes],
        *[v((3, n, 128), BF16) for n in sizes],
        v((3, 128, 512), F32), v((512, 128), F32), v((4, 8, 128), F32), v((4, 3, 8, 128), F32),
        v((128, 512), F32), v((64, 512), F32), v((128, 512), BF16), v((1024, 1024), BF16),
        v((8, 128, 128), F32), v((8, 128, 128), BF16), v((7, 128, 128), BF16),
        v((32, 512, 128), BF16), v((32, 512, 128), BF16), v((4, 32, 1024), BF16), v((4, 32, 128), BF16), v((128, 1024), BF16),
        v((1024, 128), F32), v((256, 128), F32), v((1024, 128), F32), v((1024, 128), F32), v((32, 32, 128), F32), v((32, 32, 128), F32),
        sem((13,)), sem((4,)), sem((4,)), sem((4,)), sem((4,)),
        sem((3,)), sem((4, 3)), sem((3,)), sem((4, 3)), sem((3,)), sem((3,)),
        sem((4,)), sem((4,)), sem((8,)), sem((8,)), sem((1,)), sem((1,)), sem((1,)), sem((1,)), sem((1,)), sem((1,)),
    ]


def on_device(
    acts, cotangent, master, moment1, moment2, hidden_in, k_cache, v_cache, k_new, queries, cache_len
):
    place = pl.BlockSpec(memory_space=pl.ANY)
    new_master, out = pl.pallas_call(
        kernel,
        name="update_and_decode",
        out_shape=(jax.ShapeDtypeStruct((64, 1024), F32), jax.ShapeDtypeStruct((4, 32, 1024), BF16)),
        in_specs=[pl.BlockSpec(memory_space=pltpu.SMEM)] + [place] * 10,
        out_specs=(pl.BlockSpec(memory_space=pltpu.VMEM), pl.BlockSpec(memory_space=pltpu.VMEM)),
        scratch_shapes=scratch(),
        compiler_params=pltpu.CompilerParams(
            collective_id=0, has_side_effects=True, vmem_limit_bytes=60 * 2**20
        ),
    )(
        cache_len[0], acts, cotangent, master, moment1, moment2, hidden_in.reshape(128, 1024),
        k_cache[0, 0], v_cache[0, 0], k_new[:, 0, 0], queries[:, 0, 0],
    )
    return new_master, out.reshape(4, 1, 1, 32, 1024)


def solution(mesh):
    rows = P(("fsdp", "dp"), None)
    in_specs = (
        rows, rows, rows, rows, rows,
        P(None, "dp", "fsdp", None, None),
        P("dp", "fsdp", None, None, None),
        P("dp", "fsdp", None, None, None),
        P(None, "dp", "fsdp", None, None),
        P(None, "dp", "fsdp", None, None),
        P("dp", None, None),
    )
    out_specs = (rows, P(None, "dp", "fsdp", None, None))
    return jax.shard_map(on_device, mesh=mesh, in_specs=in_specs, out_specs=out_specs, check_vma=False)
```

time: 1050 us -> 129 us (0.12)
  the two profiles are of different devices: /device:TPU:1 before, /device:TPU:29 now
where the time goes in v1:
time: 129 us; the launch traced here: 128 us
  Pallas kernels  124 us (96%)
  local copies, waits for them, and re-layouts  3.34 us (3%)
    pallas_call x1, Pallas kernels, on_device(): pl.pallas_call(kernel, name='update_and_decode', out_shape=(jax.ShapeDtyp...  124 us
    unnamed x2, local copies, waits for them, and re-layouts  3.34 us

profile of v1, /device:TPU:29, one launch (start us, length us, event | category | flops | bytes accessed | tf_op | source)
XLA Modules:
  0.0 128.4 jit_solution(1693089769633370817)
XLA Ops:
  0.6 124.4 %update_and_decode.1 = (f32[64,1024]{1,0:T(8,128)}, bf16[4,32,1024]{2,1,0:T(8,128)(2,1)}) custom-call(s32[4,32]{1,0:T(4,128)} %bitcast.15, bf16[512,8192]{1,0:T(8,128)(2,1)} %acts.1, bf16[512,1024]{1,0:T(8,128)(2,1)} %cot.1, f32[64,1024]{1,0:T(8,128)} %master.1, f32[64,1024]{1,0:T(8,128)} %mom1.1, f32[64,1024]{1,0:T(8,128)} %mom2.1, ...), custom_call_target="tpu_custom_call" | custom-call | tf_op jit(solution)/shard_map/update_and_decode/pallas_call | solution.py:384
  125.0 1.7 %copy.16 = f32[64,1024]{1,0:T(8,128)} copy(f32[64,1024]{1,0:T(8,128)} %get-tuple-element.10) | data formatting | bytes 524288
  126.7 1.7 %copy.17 = bf16[4,1,1,32,1024]{4,3,2,1,0:T(8,128)(2,1)} copy(bf16[4,1,1,32,1024]{4,3,2,1,0:T(8,128)(2,1)} %bitcast.13) | data formatting | bytes 524288

commit v2 on v1

--- a/solution.py
+++ b/solution.py
@@ -31,17 +31,19 @@
 def kernel(
     lens, acts, cot, master, mom1, mom2, hid, keys, vals, knew, query,
     nm_out, at_out,
-    abuf, cbuf, ct, g0, g1, g2, ra0, ra1, ra2, s0, s1, s2, rb0, rb1, rb2, t0, t1, t2, rc0, rc1, rc2,
-    ms, gt, nsend, nrecv, nmx, nmr, wsend, wbuf, vf, vs, vr,
+    abuf, cbuf, ct, g0, g1, g2, ra0, ra1, ra2, rb0, rb1, rb2, s0, s1, s2, rc0, rc1, rc2, t0, t1, t2, rd0, rd1, rd2,
+    ms, gt, nsend, nra, nrb, nmx, nmr, wsend, wbuf, vs, vr,
     kbuf, vbuf, qbuf, knbuf, hbuf, qs, kns, acc, ens, accn, enn,
-    loc, asend, arecv, xsend, xrecv, p1s, p1r, p2s, p2r, p3s, p3r, nss, nsr, ws, wr, fs, fr, vss, vsr, osend, orecv,
+    loc, asend, arecv, xsend, xrecv, pas, par, pbs, pbr, p2s, p2r, p3s, p3r, nss, nsr, ws, wr, hs, hr, hfs, hfr, vss, vsr, osend, orecv,
 ):
     pos, core = coordinates()
     x, y, z = pos
     other = 1 - core
     me = device(pos, core)
     sib = device(pos, other)
-    gs, ras, ss, rbs, ts, rcs = (g0, g1, g2), (ra0, ra1, ra2), (s0, s1, s2), (rb0, rb1, rb2), (t0, t1, t2), (rc0, rc1, rc2)
+    gs, ras, rbs, ss, rcs, ts, rds = (
+        (g0, g1, g2), (ra0, ra1, ra2), (rb0, rb1, rb2), (s0, s1, s2), (rc0, rc1, rc2), (t0, t1, t2), (rd0, rd1, rd2)
+    )
 
     def copy(src, dst, sem):
         return pltpu.make_async_copy(src, dst, sem)
@@ -63,12 +65,30 @@
     far = pl.ds(pl.multiple_of(other * 512, 512), 512)
     mine = pl.ds(pl.multiple_of(core * 64, 64), 64)
     theirs = pl.ds(pl.multiple_of(other * 64, 64), 64)
+
+    pair = x // 2
+    rows_here = pl.ds(pl.multiple_of(core * 128, 128), 128)
+    rows_there = pl.ds(pl.multiple_of(other * 128, 128), 128)
+
+    def mirror(p):
+        same = x // 2 == p
+        return jnp.where(same, x, 3 - x), jnp.where(same, 0, 1)
+
+    def hidden_target(yb):
+        to = (jnp.where(y // 2 == pair, y, 3 - y), yb, z)
+        group = jnp.where(y // 2 == pair, 0, 2) + x % 2
+        src = hid.at[:, pl.ds(pl.multiple_of(yb * 256, 256), 256)]
+        dst = hbuf.at[rows_here, pl.ds(pl.multiple_of(group * 256, 256), 256)]
+        return to, src, dst, (to[0] == x) & (yb == y)
 
     barrier = pltpu.get_barrier_semaphore()
     pl.semaphore_signal(barrier, inc=1, device_id=sib, device_id_type=MESH)
     for dim in range(3):
         for delta in (1, 2, 3):
             pl.semaphore_signal(barrier, inc=1, device_id=device(shifted(pos, dim, delta), core), device_id_type=MESH)
+    for delta in (1, 2, 3):
+        to = (pair * 2 + 1 - x % 2, (y + delta) % 4, z)
+        pl.semaphore_signal(barrier, inc=1, device_id=device(to, core), device_id_type=MESH)
 
     copy(cot.at[:, half], cbuf.at[0], loc.at[4]).start()
     for k in range(4):
@@ -82,9 +102,8 @@
     copy(vals, vbuf, loc.at[9]).start()
     for i, ref in enumerate((master, mom1, mom2)):
         copy(ref.at[:, half], ms.at[i, mine], loc.at[10 + i]).start()
-    copy(hid, hbuf, loc.at[5]).start()
-
-    pl.semaphore_wait(barrier, 10)
+
+    pl.semaphore_wait(barrier, 13)
 
     remote(cot.at[:, far], cbuf.at[1], xsend.at[0], xrecv.at[0], sib).start()
     for k in range(4):
@@ -92,6 +111,19 @@
         def _(j):
             to = pl.ds(pl.multiple_of(j * 128, 128), 128)
             remote(acts.at[:, lanes(k, j)], abuf.at[k, pl.ds(512, 512), to], asend.at[k], arecv.at[k], sib).start()
+
+    @pl.loop(0, 4)
+    def _(yb):
+        to, src, dst, same = hidden_target(yb)
+
+        @pl.when(jnp.logical_not(same))
+        def _():
+            remote(src, dst, hs.at[yb], hr.at[0], device(to, core)).start()
+
+        @pl.when(same)
+        def _():
+            copy(src, dst, hr.at[0]).start()
+
     for i, ref in enumerate((master, mom1, mom2)):
         remote(ref.at[:, far], ms.at[i, mine], xsend.at[1 + i], xrecv.at[1 + i], sib).start()
 
@@ -100,29 +132,48 @@
     drain(cbuf.at[1], xrecv.at[0])
     ct[:, 512:1024] = cbuf[1].T
 
+    def pass_on(k):
+        for p in range(3):
+            g, ra, rb = gs[p], ras[p], rbs[p]
+            up, down = shifted(pos, p, 1), shifted(pos, p, 3)
+            drain(ra.at[k], par.at[k, p])
+
+            @pl.loop(0, 2)
+            def _(i):
+                g[k, up[p], i] = (g[k, up[p], i].astype(F32) + ra[k, 0, i].astype(F32)).astype(BF16)
+                g[k, down[p], 2 + i] = (g[k, down[p], 2 + i].astype(F32) + ra[k, 1, i].astype(F32)).astype(BF16)
+
+            remote(g.at[k, up[p], 0:2], rb.at[k, 0, 0:2], pbs.at[p], pbr.at[k, p], device(up, core)).start()
+            remote(g.at[k, down[p], 2:4], rb.at[k, 1, 2:4], pbs.at[p], pbr.at[k, p], device(down, core)).start()
+
     for k in range(4):
         drain(abuf.at[k, pl.ds(0, 512)], loc.at[k])
         drain(abuf.at[k, pl.ds(512, 512)], arecv.at[k])
 
-        @pl.loop(0, 8)
-        def _(jp):
-            cols = pl.ds(pl.multiple_of(jp * 256, 256), 256)
+        @pl.loop(0, 4)
+        def _(xb):
+            cols = pl.ds(pl.multiple_of(xb * 512, 512), 512)
             res = jnp.dot(ct[...], abuf[k, :, cols], preferred_element_type=F32).astype(BF16)
-            xb = jp // 2
-            for e in range(2):
-                yb = (jp % 2) * 2 + e
+            for yb in range(4):
                 zb = (k + 8 - xb - yb) % 4
-                piece = res[:, e * 128 : (e + 1) * 128]
+                piece = res[:, yb * 128 : (yb + 1) * 128]
                 g0[k, xb, yb] = piece[0:176]
                 g1[k, yb, zb] = piece[176:352]
                 g2[k, zb, xb] = piece[352:512]
 
         for p in range(3):
-            for delta in (1, 2, 3):
-                to = shifted(pos, p, delta)
-                remote(
-                    gs[p].at[k, to[p]], ras[p].at[k, delta - 1], p1s.at[p], p1r.at[k, p], device(to, core)
-                ).start()
+            g, ra, rb = gs[p], ras[p], rbs[p]
+            up, down, opposite = shifted(pos, p, 1), shifted(pos, p, 3), (pos[p] + 2) % 4
+            to_up, to_down = device(up, core), device(down, core)
+            remote(g.at[k, opposite, 0:2], ra.at[k, 0], pas.at[p], par.at[k, p], to_up).start()
+            remote(g.at[k, opposite, 2:4], ra.at[k, 1], pas.at[p], par.at[k, p], to_down).start()
+            remote(g.at[k, up[p], 2:4], rb.at[k, 0, 2:4], pbs.at[p], pbr.at[k, p], to_up).start()
+            remote(g.at[k, down[p], 0:2], rb.at[k, 1, 0:2], pbs.at[p], pbr.at[k, p], to_down).start()
+        if k > 0:
+            pass_on(k - 1)
+
+    drain(hbuf.at[rows_here], hr.at[0])
+    remote(hbuf.at[rows_here], hbuf.at[rows_here], hfs.at[0], hfr.at[0], sib).start()
 
     copy(query, qbuf, loc.at[6]).wait()
     copy(knew, knbuf, loc.at[7]).wait()
@@ -164,28 +215,26 @@
     def first_sum(k):
         for p in range(3):
             b = (p + 1) % 3
-            drain(ras[p].at[k], p1r.at[k, p])
+            drain(rbs[p].at[k], pbr.at[k, p])
 
             @pl.loop(0, 4)
             def _(i):
-                total = gs[p][k, pos[p], i].astype(F32)
-                for slot in range(3):
-                    total += ras[p][k, slot, i].astype(F32)
+                total = gs[p][k, pos[p], i].astype(F32) + rbs[p][k, 0, i].astype(F32) + rbs[p][k, 1, i].astype(F32)
                 ss[p][k, i] = total.astype(BF16)
 
             for delta in (1, 2, 3):
                 to = shifted(pos, b, delta)
                 remote(
-                    ss[p].at[k, to[b]], rbs[p].at[k, delta - 1], p2s.at[p], p2r.at[k, p], device(to, core)
+                    ss[p].at[k, to[b]], rcs[p].at[k, delta - 1], p2s.at[p], p2r.at[k, p], device(to, core)
                 ).start()
 
     def second_sum(k):
         for p in range(3):
             b, c = (p + 1) % 3, (p + 2) % 3
-            drain(rbs[p].at[k], p2r.at[k, p])
+            drain(rcs[p].at[k], p2r.at[k, p])
             total = ss[p][k, pos[b]].astype(F32)
             for slot in range(3):
-                total += rbs[p][k, slot].astype(F32)
+                total += rcs[p][k, slot].astype(F32)
             ts[p][k] = total.astype(BF16)
             target = (k + 8 - pos[p] - pos[b]) % 4
             delta = (target + 4 - pos[c]) % 4
@@ -193,10 +242,11 @@
             @pl.when(delta != 0)
             def _():
                 remote(
-                    ts[p].at[k], rcs[p].at[delta - 1], p3s.at[p], p3r.at[p], device(shifted(pos, c, delta), core)
+                    ts[p].at[k], rds[p].at[delta - 1], p3s.at[p], p3r.at[p], device(shifted(pos, c, delta), core)
                 ).start()
 
     attend_rows(0)
+    pass_on(3)
     first_sum(0)
     attend_rows(8)
     first_sum(1)
@@ -214,31 +264,30 @@
 
     own = (x + y + z) % 4
     for p, (first, size) in enumerate(PARTS):
-        drain(rcs[p], p3r.at[p])
+        drain(rds[p], p3r.at[p])
         total = ts[p][own].astype(F32)
         for slot in range(3):
-            total += rcs[p][slot].astype(F32)
+            total += rds[p][slot].astype(F32)
         gt[pl.ds(first, size), :] = total
 
     square = jnp.zeros((8, 128), F32)
     for i in range(64):
         part = gt[pl.ds(i * 8, 8), :]
         square += part * part
-    for stage in range(4):
-        nsend[stage] = square
-        if stage == 0:
-            remote(nsend.at[0], nrecv.at[0, 0], nss.at[0], nsr.at[0], sib).start()
-            drain(nrecv.at[0, 0], nsr.at[0])
-            square += nrecv[0, 0]
-        else:
-            for delta in (1, 2, 3):
-                remote(
-                    nsend.at[stage], nrecv.at[stage, delta - 1], nss.at[stage], nsr.at[stage],
-                    device(shifted(pos, stage - 1, delta), core),
-                ).start()
-            drain(nrecv.at[stage], nsr.at[stage])
-            for slot in range(3):
-                square += nrecv[stage, slot]
+    nsend[0] = square
+    for q in range(1, 8):
+        to = device(((x + q // 2) % 4, y, z), (core + q) % 2)
+        remote(nsend.at[0], nra.at[q - 1], nss.at[0], nsr.at[0], to).start()
+    drain(nra, nsr.at[0])
+    for slot in range(7):
+        square += nra[slot]
+    nsend[1] = square
+    for q in range(1, 16):
+        to = device((x, (y + q // 4) % 4, (z + q) % 4), core)
+        remote(nsend.at[1], nrb.at[q - 1], nss.at[1], nsr.at[1], to).start()
+    drain(nrb, nsr.at[1])
+    for slot in range(15):
+        square += nrb[slot]
     gnorm = jnp.sqrt(jnp.sum(square, keepdims=True))
     clip = jnp.minimum(1.0, 1.0 / (gnorm + 1e-06))
 
@@ -256,69 +305,58 @@
         nmx[:, cols] = weights
         wsend[:, cols] = weights.astype(BF16)
 
-    place = pl.ds(pl.multiple_of((y * 2 + z // 2) * 128, 128), 128)
-    number = (y % 2) * 4 + (z // 2) * 2 + core
-    to_core = y // 2
-
-    def target(q):
-        to = ((z % 2) + 2 * (q // 4), x, (z + q) % 4)
-        same = (to[0] == x) & (to[1] == y) & (to[2] == z) & (to_core == core)
-        return device(to, to_core), same
+    def weight_target(q):
+        xb, far_pair = mirror(q // 4)
+        zb = (z + q) % 4
+        slot = far_pair * 4 + (z % 2) * 2 + z // 2
+        dst = wbuf.at[pl.ds(pl.multiple_of(slot * 128, 128), 128), :]
+        return (xb, y, zb), dst, (xb == x) & (zb == z)
 
     @pl.loop(0, 8)
     def _(q):
-        dev, same = target(q)
+        to, dst, same = weight_target(q)
 
         @pl.when(jnp.logical_not(same))
         def _():
-            remote(wsend, wbuf.at[place, half], ws.at[q], wr.at[number], dev).start()
+            remote(wsend, dst, ws.at[q], wr.at[0], device(to, core)).start()
 
         @pl.when(same)
         def _():
-            copy(wsend, wbuf.at[place, half], wr.at[number]).start()
+            copy(wsend, dst, wr.at[0]).start()
 
     remote(nmx.at[theirs], nmr, osend.at[0], orecv.at[0], sib).start()
     nm_out[:, half] = nmx[mine, :]
-    copy(hid, hbuf, loc.at[5]).wait()
-
-    @pl.loop(0, 8)
-    def _(sl):
-        rows = pl.ds(pl.multiple_of(((2 * core + sl // 4) * 2 + (sl // 2) % 2) * 128, 128), 128)
-        cols = pl.ds(pl.multiple_of((sl % 2) * 512, 512), 512)
-        drain(wbuf.at[rows, cols], wr.at[sl])
-        remote(wbuf.at[rows, cols], wbuf.at[rows, cols], fs.at[0], fr.at[0], sib).start()
-
-    @pl.loop(0, 4)
-    def _(n):
-        cols = pl.ds(pl.multiple_of(n * 256, 256), 256)
-        res = jnp.dot(hbuf[:, half], wbuf[half, cols], preferred_element_type=F32)
-        vf[2 * n] = res[:, 0:128]
-        vf[2 * n + 1] = res[:, 128:256]
-
+    drain(hbuf.at[rows_there], hfr.at[0])
     drain(nmr, orecv.at[0])
     nm_out[:, far] = nmr[...]
-    drain(wbuf.at[far], fr.at[0])
-    head = (x % 2) * 4 + y
-
-    @pl.loop(0, 4)
-    def _(n):
-        cols = pl.ds(pl.multiple_of(n * 256, 256), 256)
-        res = jnp.dot(hbuf[:, far], wbuf[far, cols], preferred_element_type=F32)
+    drain(wbuf, wr.at[0])
+
+    number = (x % 2) * 4 + y
+
+    def value_target(q):
+        to = (pair * 2 + core, q // 2, z)
+        to_core = q % 2
+        return to, to_core, (to[0] == x) & (to[1] == y) & (to_core == core)
+
+    for n in range(2):
+        res = jnp.dot(hbuf[...], wbuf[:, n * 256 : (n + 1) * 256], preferred_element_type=F32).astype(BF16)
         for e in range(2):
-            to_head = 2 * n + e
-            total = vf[to_head] + res[:, e * 128 : (e + 1) * 128]
-            vf[to_head] = total
-            vs[to_head] = total.astype(BF16)
-            delta = (to_head + 8 - head) % 8
-            to = ((x // 2) * 2 + to_head // 4, to_head % 4, z)
-
-            @pl.when(delta != 0)
-            def _():
-                remote(vs.at[to_head], vr.at[delta - 1], vss.at[0], vsr.at[0], device(to, core)).start()
+            for c in range(2):
+                q = (n * 2 + e) * 2 + c
+                vs[q] = res[c * 128 : (c + 1) * 128, e * 128 : (e + 1) * 128]
+                to, to_core, same = value_target(q)
+
+                @pl.when(jnp.logical_not(same))
+                def _():
+                    remote(vs.at[q], vr.at[number], vss.at[q], vsr.at[0], device(to, to_core)).start()
+
+                @pl.when(same)
+                def _():
+                    copy(vs.at[q], vr.at[number], vsr.at[0]).start()
 
     drain(vr, vsr.at[0])
-    total = vf[head]
-    for slot in range(7):
+    total = vr[0].astype(F32)
+    for slot in range(1, 8):
         total += vr[slot].astype(F32)
     vnew = (total * (32.0 * 8192 ** (-0.5))).astype(BF16).astype(F32)
     for s in range(4):
@@ -335,24 +373,37 @@
     for k in range(4):
         drain(abuf.at[k, pl.ds(512, 512)], asend.at[k])
     for p in range(3):
-        drain(ras[p], p1s.at[p])
-        drain(rbs[p], p2s.at[p])
-        drain(rcs[p], p3s.at[p])
-    drain(nrecv.at[0, 0], nss.at[0])
-    for stage in range(1, 4):
-        drain(nrecv.at[stage], nss.at[stage])
+        drain(ras[p], pas.at[p])
+        drain(rbs[p], pbs.at[p])
+        drain(rcs[p], p2s.at[p])
+        drain(rds[p], p3s.at[p])
+    drain(nra, nss.at[0])
+    drain(nrb, nss.at[1])
 
     @pl.loop(0, 8)
     def _(q):
-        _, same = target(q)
+        _, _, same = weight_target(q)
 
         @pl.when(jnp.logical_not(same))
         def _():
             drain(wsend, ws.at[q])
 
+        _, _, same_value = value_target(q)
+
+        @pl.when(jnp.logical_not(same_value))
+        def _():
+            drain(vs.at[q], vss.at[q])
+
+    @pl.loop(0, 4)
+    def _(yb):
+        _, _, dst, same = hidden_target(yb)
+
+        @pl.when(jnp.logical_not(same))
+        def _():
+            drain(dst, hs.at[yb])
+
     drain(nmr, osend.at[0])
-    drain(wbuf.at[half], fs.at[0])
-    drain(vr, vss.at[0])
+    drain(hbuf.at[rows_here], hfs.at[0])
 
 
 def scratch():
@@ -361,19 +412,20 @@
     return [
         v((4, 1024, 2048), BF16), v((2, 512, 512), BF16), v((512, 1024), BF16),
         *[v((4, 4, 4, n, 128), BF16) for n in sizes],
-        *[v((4, 3, 4, n, 128), BF16) for n in sizes],
+        *[v((4, 2, 2, n, 128), BF16) for n in sizes],
+        *[v((4, 2, 4, n, 128), BF16) for n in sizes],
         *[v((4, 4, n, 128), BF16) for n in sizes],
         *[v((4, 3, n, 128), BF16) for n in sizes],
         *[v((4, n, 128), BF16) for n in sizes],
         *[v((3, n, 128), BF16) for n in sizes],
-        v((3, 128, 512), F32), v((512, 128), F32), v((4, 8, 128), F32), v((4, 3, 8, 128), F32),
-        v((128, 512), F32), v((64, 512), F32), v((128, 512), BF16), v((1024, 1024), BF16),
-        v((8, 128, 128), F32), v((8, 128, 128), BF16), v((7, 128, 128), BF16),
-        v((32, 512, 128), BF16), v((32, 512, 128), BF16), v((4, 32, 1024), BF16), v((4, 32, 128), BF16), v((128, 1024), BF16),
+        v((3, 128, 512), F32), v((512, 128), F32), v((2, 8, 128), F32), v((7, 8, 128), F32), v((15, 8, 128), F32),
+        v((128, 512), F32), v((64, 512), F32), v((128, 512), BF16), v((1024, 512), BF16),
+        v((8, 128, 128), BF16), v((8, 128, 128), BF16),
+        v((32, 512, 128), BF16), v((32, 512, 128), BF16), v((4, 32, 1024), BF16), v((4, 32, 128), BF16), v((256, 1024), BF16),
         v((1024, 128), F32), v((256, 128), F32), v((1024, 128), F32), v((1024, 128), F32), v((32, 32, 128), F32), v((32, 32, 128), F32),
         sem((13,)), sem((4,)), sem((4,)), sem((4,)), sem((4,)),
-        sem((3,)), sem((4, 3)), sem((3,)), sem((4, 3)), sem((3,)), sem((3,)),
-        sem((4,)), sem((4,)), sem((8,)), sem((8,)), sem((1,)), sem((1,)), sem((1,)), sem((1,)), sem((1,)), sem((1,)),
+        sem((3,)), sem((4, 3)), sem((3,)), sem((4, 3)), sem((3,)), sem((4, 3)), sem((3,)), sem((3,)),
+        sem((2,)), sem((2,)), sem((8,)), sem((1,)), sem((4,)), sem((1,)), sem((1,)), sem((1,)), sem((8,)), sem((1,)), sem((1,)), sem((1,)),
     ]
 
 

time: 129 us -> 95.1 us (0.74)
  the two profiles are of different devices: /device:TPU:29 before, /device:TPU:1 now
where the time goes in v2:
time: 95.1 us; the launch traced here: 94.9 us
  Pallas kernels  90.9 us (96%)
  local copies, waits for them, and re-layouts  3.34 us (4%)
    pallas_call x1, Pallas kernels, on_device(): pl.pallas_call(kernel, name='update_and_decode', out_shape=(jax.ShapeDtyp...  90.9 us
    unnamed x2, local copies, waits for them, and re-layouts  3.34 us

profile of v2, /device:TPU:1, one launch (start us, length us, event | category | flops | bytes accessed | tf_op | source)
XLA Modules:
  0.0 94.9 jit_solution(18315302367096034360)
XLA Ops:
  0.6 90.9 %update_and_decode.1 = (f32[64,1024]{1,0:T(8,128)}, bf16[4,32,1024]{2,1,0:T(8,128)(2,1)}) custom-call(s32[4,32]{1,0:T(4,128)} %bitcast.15, bf16[512,8192]{1,0:T(8,128)(2,1)} %acts.1, bf16[512,1024]{1,0:T(8,128)(2,1)} %cot.1, f32[64,1024]{1,0:T(8,128)} %master.1, f32[64,1024]{1,0:T(8,128)} %mom1.1, f32[64,1024]{1,0:T(8,128)} %mom2.1, ...), custom_call_target="tpu_custom_call" | custom-call | tf_op jit(solution)/shard_map/update_and_decode/pallas_call | solution.py:436
  91.6 1.7 %copy.16 = f32[64,1024]{1,0:T(8,128)} copy(f32[64,1024]{1,0:T(8,128)} %get-tuple-element.10) | data formatting | bytes 524288
  93.2 1.7 %copy.17 = bf16[4,1,1,32,1024]{4,3,2,1,0:T(8,128)(2,1)} copy(bf16[4,1,1,32,1024]{4,3,2,1,0:T(8,128)(2,1)} %bitcast.13) | data formatting | bytes 524288

commit v3 on v2

--- a/solution.py
+++ b/solution.py
@@ -66,29 +66,22 @@
     mine = pl.ds(pl.multiple_of(core * 64, 64), 64)
     theirs = pl.ds(pl.multiple_of(other * 64, 64), 64)
 
-    pair = x // 2
-    rows_here = pl.ds(pl.multiple_of(core * 128, 128), 128)
-    rows_there = pl.ds(pl.multiple_of(other * 128, 128), 128)
-
-    def mirror(p):
-        same = x // 2 == p
-        return jnp.where(same, x, 3 - x), jnp.where(same, 0, 1)
+    tokens_here = pl.ds(pl.multiple_of(core * 256, 256), 256)
+    tokens_there = pl.ds(pl.multiple_of(other * 256, 256), 256)
 
     def hidden_target(yb):
-        to = (jnp.where(y // 2 == pair, y, 3 - y), yb, z)
-        group = jnp.where(y // 2 == pair, 0, 2) + x % 2
         src = hid.at[:, pl.ds(pl.multiple_of(yb * 256, 256), 256)]
-        dst = hbuf.at[rows_here, pl.ds(pl.multiple_of(group * 256, 256), 256)]
-        return to, src, dst, (to[0] == x) & (yb == y)
+        dst = hbuf.at[
+            pl.ds(pl.multiple_of(core * 256 + (x // 2) * 128, 128), 128),
+            pl.ds(pl.multiple_of((x % 2) * 256, 256), 256),
+        ]
+        return (y, yb, z), src, dst, (y == x) & (yb == y)
 
     barrier = pltpu.get_barrier_semaphore()
     pl.semaphore_signal(barrier, inc=1, device_id=sib, device_id_type=MESH)
     for dim in range(3):
         for delta in (1, 2, 3):
             pl.semaphore_signal(barrier, inc=1, device_id=device(shifted(pos, dim, delta), core), device_id_type=MESH)
-    for delta in (1, 2, 3):
-        to = (pair * 2 + 1 - x % 2, (y + delta) % 4, z)
-        pl.semaphore_signal(barrier, inc=1, device_id=device(to, core), device_id_type=MESH)
 
     copy(cot.at[:, half], cbuf.at[0], loc.at[4]).start()
     for k in range(4):
@@ -96,33 +89,21 @@
         def _(j):
             to = pl.ds(pl.multiple_of(j * 128, 128), 128)
             copy(acts.at[:, lanes(k, j)], abuf.at[k, pl.ds(0, 512), to], loc.at[k]).start()
+
     copy(query, qbuf, loc.at[6]).start()
     copy(knew, knbuf, loc.at[7]).start()
     copy(keys, kbuf, loc.at[8]).start()
     copy(vals, vbuf, loc.at[9]).start()
     for i, ref in enumerate((master, mom1, mom2)):
         copy(ref.at[:, half], ms.at[i, mine], loc.at[10 + i]).start()
-
-    pl.semaphore_wait(barrier, 13)
+    pl.semaphore_wait(barrier, 10)
 
     remote(cot.at[:, far], cbuf.at[1], xsend.at[0], xrecv.at[0], sib).start()
     for k in range(4):
         @pl.loop(0, 16)
         def _(j):
             to = pl.ds(pl.multiple_of(j * 128, 128), 128)
-            remote(acts.at[:, lanes(k, j)], abuf.at[k, pl.ds(512, 512), to], asend.at[k], arecv.at[k], sib).start()
-
-    @pl.loop(0, 4)
-    def _(yb):
-        to, src, dst, same = hidden_target(yb)
-
-        @pl.when(jnp.logical_not(same))
-        def _():
-            remote(src, dst, hs.at[yb], hr.at[0], device(to, core)).start()
-
-        @pl.when(same)
-        def _():
-            copy(src, dst, hr.at[0]).start()
+            remote(acts.at[:, lanes(k, j)], abuf.at[k, pl.ds(512, 512), to], asend.at[k], arecv.at[k, j // 4], sib).start()
 
     for i, ref in enumerate((master, mom1, mom2)):
         remote(ref.at[:, far], ms.at[i, mine], xsend.at[1 + i], xrecv.at[1 + i], sib).start()
@@ -148,11 +129,10 @@
 
     for k in range(4):
         drain(abuf.at[k, pl.ds(0, 512)], loc.at[k])
-        drain(abuf.at[k, pl.ds(512, 512)], arecv.at[k])
-
         @pl.loop(0, 4)
         def _(xb):
             cols = pl.ds(pl.multiple_of(xb * 512, 512), 512)
+            drain(abuf.at[k, pl.ds(512, 512), cols], arecv.at[k, xb])
             res = jnp.dot(ct[...], abuf[k, :, cols], preferred_element_type=F32).astype(BF16)
             for yb in range(4):
                 zb = (k + 8 - xb - yb) % 4
@@ -172,8 +152,6 @@
         if k > 0:
             pass_on(k - 1)
 
-    drain(hbuf.at[rows_here], hr.at[0])
-    remote(hbuf.at[rows_here], hbuf.at[rows_here], hfs.at[0], hfr.at[0], sib).start()
 
     copy(query, qbuf, loc.at[6]).wait()
     copy(knew, knbuf, loc.at[7]).wait()
@@ -206,8 +184,8 @@
         acc[rows, :] = out * inv
         ens[rows, 0:8] = en.astype(BF16).astype(F32) * inv
 
-    def attend_rows(first):
-        @pl.loop(0, 4)
+    def attend_rows(first, pairs=4):
+        @pl.loop(0, pairs)
         def _(i):
             attend(first + 2 * i)
             attend(first + 2 * i + 1)
@@ -245,8 +223,9 @@
                     ts[p].at[k], rds[p].at[delta - 1], p3s.at[p], p3r.at[p], device(shifted(pos, c, delta), core)
                 ).start()
 
-    attend_rows(0)
+    attend_rows(0, 2)
     pass_on(3)
+    attend_rows(4, 2)
     first_sum(0)
     attend_rows(8)
     first_sum(1)
@@ -254,10 +233,6 @@
     attend_rows(16)
     first_sum(2)
     second_sum(1)
-    attend_rows(24)
-    for j in range(32):
-        accn[j] = acc[pl.ds(j, 32, stride=32), :]
-        enn[j] = ens[pl.ds(j, 32, stride=32), :]
     first_sum(3)
     second_sum(2)
     second_sum(3)
@@ -278,6 +253,7 @@
     for q in range(1, 8):
         to = device(((x + q // 2) % 4, y, z), (core + q) % 2)
         remote(nsend.at[0], nra.at[q - 1], nss.at[0], nsr.at[0], to).start()
+    attend_rows(24, 2)
     drain(nra, nsr.at[0])
     for slot in range(7):
         square += nra[slot]
@@ -285,6 +261,22 @@
     for q in range(1, 16):
         to = device((x, (y + q // 4) % 4, (z + q) % 4), core)
         remote(nsend.at[1], nrb.at[q - 1], nss.at[1], nsr.at[1], to).start()
+    @pl.loop(0, 4)
+    def _(yb):
+        to, src, dst, same = hidden_target(yb)
+
+        @pl.when(jnp.logical_not(same))
+        def _():
+            remote(src, dst, hs.at[yb], hr.at[0], device(to, core)).start()
+
+        @pl.when(same)
+        def _():
+            copy(src, dst, hr.at[0]).start()
+
+    attend_rows(28, 2)
+    for j in range(32):
+        accn[j] = acc[pl.ds(j, 32, stride=32), :]
+        enn[j] = ens[pl.ds(j, 32, stride=32), :]
     drain(nrb, nsr.at[1])
     for slot in range(15):
         square += nrb[slot]
@@ -294,6 +286,7 @@
     for i in range(3):
         drain(ms.at[i, mine], loc.at[10 + i])
         drain(ms.at[i, theirs], xrecv.at[1 + i])
+    place = pl.ds(pl.multiple_of(((z % 2) * 2 + z // 2) * 128, 128), 128)
     for j in range(4):
         cols = slice(j * 128, (j + 1) * 128)
         clipped = gt[pl.ds(j * 128, 128), :].T * clip
@@ -303,52 +296,34 @@
         weights = ms[0, :, cols]
         weights = weights - 0.1 * (update + 0.1 * weights)
         nmx[:, cols] = weights
-        wsend[:, cols] = weights.astype(BF16)
-
-    def weight_target(q):
-        xb, far_pair = mirror(q // 4)
-        zb = (z + q) % 4
-        slot = far_pair * 4 + (z % 2) * 2 + z // 2
-        dst = wbuf.at[pl.ds(pl.multiple_of(slot * 128, 128), 128), :]
-        return (xb, y, zb), dst, (xb == x) & (zb == z)
-
-    @pl.loop(0, 8)
-    def _(q):
-        to, dst, same = weight_target(q)
-
-        @pl.when(jnp.logical_not(same))
-        def _():
-            remote(wsend, dst, ws.at[q], wr.at[0], device(to, core)).start()
-
-        @pl.when(same)
-        def _():
-            copy(wsend, dst, wr.at[0]).start()
-
+        wsend[j] = weights.astype(BF16)
+        for q in (2, 1, 3):
+            to = (x, y, (z + q) % 4)
+            remote(wsend.at[j], wbuf.at[j, place], ws.at[0], wr.at[j], device(to, core)).start()
+        copy(wsend.at[j], wbuf.at[j, place], wr.at[j]).start()
+
+    drain(hbuf.at[tokens_here], hr.at[0])
+    remote(hbuf.at[tokens_here], hbuf.at[tokens_here], hfs.at[0], hfr.at[0], sib).start()
     remote(nmx.at[theirs], nmr, osend.at[0], orecv.at[0], sib).start()
     nm_out[:, half] = nmx[mine, :]
-    drain(hbuf.at[rows_there], hfr.at[0])
+    drain(hbuf.at[tokens_there], hfr.at[0])
     drain(nmr, orecv.at[0])
     nm_out[:, far] = nmr[...]
-    drain(wbuf, wr.at[0])
-
-    number = (x % 2) * 4 + y
-
-    def value_target(q):
-        to = (pair * 2 + core, q // 2, z)
-        to_core = q % 2
-        return to, to_core, (to[0] == x) & (to[1] == y) & (to_core == core)
-
-    for n in range(2):
-        res = jnp.dot(hbuf[...], wbuf[:, n * 256 : (n + 1) * 256], preferred_element_type=F32).astype(BF16)
-        for e in range(2):
+
+    number = x * 4 + y
+    for j in range(4):
+        drain(wbuf.at[j], wr.at[j])
+        res = jnp.dot(hbuf[...], wbuf[j], preferred_element_type=F32).astype(BF16)
+        for xp in range(2):
             for c in range(2):
-                q = (n * 2 + e) * 2 + c
-                vs[q] = res[c * 128 : (c + 1) * 128, e * 128 : (e + 1) * 128]
-                to, to_core, same = value_target(q)
+                q = j * 4 + xp * 2 + c
+                vs[q] = res[c * 256 + xp * 128 : c * 256 + (xp + 1) * 128]
+                to = (xp * 2 + core, j, z)
+                same = (to[0] == x) & (to[1] == y) & (c == core)
 
                 @pl.when(jnp.logical_not(same))
                 def _():
-                    remote(vs.at[q], vr.at[number], vss.at[q], vsr.at[0], device(to, to_core)).start()
+                    remote(vs.at[q], vr.at[number], vss.at[q], vsr.at[0], device(to, c)).start()
 
                 @pl.when(same)
                 def _():
@@ -356,7 +331,7 @@
 
     drain(vr, vsr.at[0])
     total = vr[0].astype(F32)
-    for slot in range(1, 8):
+    for slot in range(1, 16):
         total += vr[slot].astype(F32)
     vnew = (total * (32.0 * 8192 ** (-0.5))).astype(BF16).astype(F32)
     for s in range(4):
@@ -380,17 +355,13 @@
     drain(nra, nss.at[0])
     drain(nrb, nss.at[1])
 
-    @pl.loop(0, 8)
+    drain(wbuf.at[:, pl.ds(0, 384)], ws.at[0])
+
+    @pl.loop(0, 16)
     def _(q):
-        _, _, same = weight_target(q)
+        same = ((q // 2) % 2 * 2 + core == x) & (q // 4 == y) & (q % 2 == core)
 
         @pl.when(jnp.logical_not(same))
-        def _():
-            drain(wsend, ws.at[q])
-
-        _, _, same_value = value_target(q)
-
-        @pl.when(jnp.logical_not(same_value))
         def _():
             drain(vs.at[q], vss.at[q])
 
@@ -403,7 +374,7 @@
             drain(dst, hs.at[yb])
 
     drain(nmr, osend.at[0])
-    drain(hbuf.at[rows_here], hfs.at[0])
+    drain(hbuf.at[tokens_here], hfs.at[0])
 
 
 def scratch():
@@ -419,13 +390,13 @@
         *[v((4, n, 128), BF16) for n in sizes],
         *[v((3, n, 128), BF16) for n in sizes],
         v((3, 128, 512), F32), v((512, 128), F32), v((2, 8, 128), F32), v((7, 8, 128), F32), v((15, 8, 128), F32),
-        v((128, 512), F32), v((64, 512), F32), v((128, 512), BF16), v((1024, 512), BF16),
-        v((8, 128, 128), BF16), v((8, 128, 128), BF16),
-        v((32, 512, 128), BF16), v((32, 512, 128), BF16), v((4, 32, 1024), BF16), v((4, 32, 128), BF16), v((256, 1024), BF16),
+        v((128, 512), F32), v((64, 512), F32), v((4, 128, 128), BF16), v((4, 512, 128), BF16),
+        v((16, 128, 128), BF16), v((16, 128, 128), BF16),
+        v((32, 512, 128), BF16), v((32, 512, 128), BF16), v((4, 32, 1024), BF16), v((4, 32, 128), BF16), v((512, 512), BF16),
         v((1024, 128), F32), v((256, 128), F32), v((1024, 128), F32), v((1024, 128), F32), v((32, 32, 128), F32), v((32, 32, 128), F32),
-        sem((13,)), sem((4,)), sem((4,)), sem((4,)), sem((4,)),
+        sem((13,)), sem((4,)), sem((4, 4)), sem((4,)), sem((4,)),
         sem((3,)), sem((4, 3)), sem((3,)), sem((4, 3)), sem((3,)), sem((4, 3)), sem((3,)), sem((3,)),
-        sem((2,)), sem((2,)), sem((8,)), sem((1,)), sem((4,)), sem((1,)), sem((1,)), sem((1,)), sem((8,)), sem((1,)), sem((1,)), sem((1,)),
+        sem((2,)), sem((2,)), sem((1,)), sem((4,)), sem((4,)), sem((1,)), sem((1,)), sem((1,)), sem((16,)), sem((1,)), sem((1,)), sem((1,)),
     ]
 
 

time: 95.1 us -> 89.1 us (0.937)
  Pallas kernels: 90.9 us -> 84.9 us
    pallas_call x1, Pallas kernels: 90.9 us -> 84.9 us  [on_device(): pl.pallas_call(kernel, name='update_and_decode', out_shape=(jax.ShapeDtyp...]
where the time goes in v3:
time: 89.1 us; the launch traced here: 88.9 us
  Pallas kernels  84.9 us (95%)
  local copies, waits for them, and re-layouts  3.34 us (4%)
    pallas_call x1, Pallas kernels, on_device(): pl.pallas_call(kernel, name='update_and_decode', out_shape=(jax.ShapeDtyp...  84.9 us
    unnamed x2, local copies, waits for them, and re-layouts  3.34 us

profile of v3, /device:TPU:1, one launch (start us, length us, event | category | flops | bytes accessed | tf_op | source)
XLA Modules:
  0.0 88.9 jit_solution(2216091011123222548)
XLA Ops:
  0.6 84.9 %update_and_decode.1 = (f32[64,1024]{1,0:T(8,128)}, bf16[4,32,1024]{2,1,0:T(8,128)(2,1)}) custom-call(s32[4,32]{1,0:T(4,128)} %bitcast.15, bf16[512,8192]{1,0:T(8,128)(2,1)} %acts.1, bf16[512,1024]{1,0:T(8,128)(2,1)} %cot.1, f32[64,1024]{1,0:T(8,128)} %master.1, f32[64,1024]{1,0:T(8,128)} %mom1.1, f32[64,1024]{1,0:T(8,128)} %mom2.1, ...), custom_call_target="tpu_custom_call" | custom-call | tf_op jit(solution)/shard_map/update_and_decode/pallas_call | solution.py:407
  85.6 1.7 %copy.16 = f32[64,1024]{1,0:T(8,128)} copy(f32[64,1024]{1,0:T(8,128)} %get-tuple-element.10) | data formatting | bytes 524288
  87.2 1.7 %copy.17 = bf16[4,1,1,32,1024]{4,3,2,1,0:T(8,128)(2,1)} copy(bf16[4,1,1,32,1024]{4,3,2,1,0:T(8,128)(2,1)} %bitcast.13) | data formatting | bytes 524288

commit v4 on v3

--- a/solution.py
+++ b/solution.py
@@ -79,8 +79,8 @@
 
     barrier = pltpu.get_barrier_semaphore()
     pl.semaphore_signal(barrier, inc=1, device_id=sib, device_id_type=MESH)
-    for dim in range(3):
-        for delta in (1, 2, 3):
+    for dim in (2, 1, 0):
+        for delta in (2, 1, 3):
             pl.semaphore_signal(barrier, inc=1, device_id=device(shifted(pos, dim, delta), core), device_id_type=MESH)
 
     copy(cot.at[:, half], cbuf.at[0], loc.at[4]).start()
@@ -230,7 +230,6 @@
     attend_rows(8)
     first_sum(1)
     second_sum(0)
-    attend_rows(16)
     first_sum(2)
     second_sum(1)
     first_sum(3)
@@ -253,7 +252,7 @@
     for q in range(1, 8):
         to = device(((x + q // 2) % 4, y, z), (core + q) % 2)
         remote(nsend.at[0], nra.at[q - 1], nss.at[0], nsr.at[0], to).start()
-    attend_rows(24, 2)
+    attend_rows(16, 4)
     drain(nra, nsr.at[0])
     for slot in range(7):
         square += nra[slot]
@@ -273,7 +272,7 @@
         def _():
             copy(src, dst, hr.at[0]).start()
 
-    attend_rows(28, 2)
+    attend_rows(24, 4)
     for j in range(32):
         accn[j] = acc[pl.ds(j, 32, stride=32), :]
         enn[j] = ens[pl.ds(j, 32, stride=32), :]
@@ -407,7 +406,7 @@
     new_master, out = pl.pallas_call(
         kernel,
         name="update_and_decode",
-        out_shape=(jax.ShapeDtypeStruct((64, 1024), F32), jax.ShapeDtypeStruct((4, 32, 1024), BF16)),
+        out_shape=(pltpu.VMEM((64, 1024), F32), pltpu.VMEM((4, 32, 1024), BF16)),
         in_specs=[pl.BlockSpec(memory_space=pltpu.SMEM)] + [place] * 10,
         out_specs=(pl.BlockSpec(memory_space=pltpu.VMEM), pl.BlockSpec(memory_space=pltpu.VMEM)),
         scratch_shapes=scratch(),

time: 89.1 us -> 84.5 us (0.948)
  Pallas kernels: 84.9 us -> 82.3 us
  local copies, waits for them, and re-layouts: 3.34 us -> 1.41 us
    pallas_call x1, Pallas kernels: 84.9 us -> 82.3 us  [on_device(): pl.pallas_call(kernel, name='update_and_decode', out_shape=(pltpu.VMEM((6...]
    unnamed x2, local copies, waits for them, and re-layouts: 3.34 us -> 1.41 us
where the time goes in v4:
time: 84.5 us; the launch traced here: 84.4 us
  Pallas kernels  82.3 us (97%)
  local copies, waits for them, and re-layouts  1.41 us (2%)
    pallas_call x1, Pallas kernels, on_device(): pl.pallas_call(kernel, name='update_and_decode', out_shape=(pltpu.VMEM((6...  82.3 us

profile of v4, /device:TPU:1, one launch (start us, length us, event | category | flops | bytes accessed | tf_op | source)
XLA Modules:
  0.0 84.4 jit_solution(3460103750555977383)
XLA Ops:
  0.6 82.3 %update_and_decode.1 = (f32[64,1024]{1,0:T(8,128)S(1)}, bf16[4,32,1024]{2,1,0:T(8,128)(2,1)S(1)}) custom-call(s32[4,32]{1,0:T(4,128)} %bitcast.15, bf16[512,8192]{1,0:T(8,128)(2,1)} %acts.1, bf16[512,1024]{1,0:T(8,128)(2,1)} %cot.1, f32[64,1024]{1,0:T(8,128)} %master.1, f32[64,1024]{1,0:T(8,128)} %mom1.1, f32[64,1024]{1,0:T(8,128)} %mom2.1, ...), custom_call_target="tpu_custom_call" | custom-call | tf_op jit(solution)/shard_map/update_and_decode/pallas_call | solution.py:406
  83.0 0.7 copy.16
  83.7 0.7 copy.17

commit v5 on v4

--- a/solution.py
+++ b/solution.py
@@ -200,7 +200,7 @@
                 total = gs[p][k, pos[p], i].astype(F32) + rbs[p][k, 0, i].astype(F32) + rbs[p][k, 1, i].astype(F32)
                 ss[p][k, i] = total.astype(BF16)
 
-            for delta in (1, 2, 3):
+            for delta in (2, 1, 3):
                 to = shifted(pos, b, delta)
                 remote(
                     ss[p].at[k, to[b]], rcs[p].at[k, delta - 1], p2s.at[p], p2r.at[k, p], device(to, core)
@@ -249,7 +249,7 @@
         part = gt[pl.ds(i * 8, 8), :]
         square += part * part
     nsend[0] = square
-    for q in range(1, 8):
+    for q in (5, 4, 3, 7, 2, 6, 1):
         to = device(((x + q // 2) % 4, y, z), (core + q) % 2)
         remote(nsend.at[0], nra.at[q - 1], nss.at[0], nsr.at[0], to).start()
     attend_rows(16, 4)
@@ -257,7 +257,7 @@
     for slot in range(7):
         square += nra[slot]
     nsend[1] = square
-    for q in range(1, 16):
+    for q in (10, 9, 11, 6, 14, 2, 8, 5, 7, 13, 15, 1, 3, 4, 12):
         to = device((x, (y + q // 4) % 4, (z + q) % 4), core)
         remote(nsend.at[1], nrb.at[q - 1], nss.at[1], nsr.at[1], to).start()
     @pl.loop(0, 4)

time: 84.5 us -> 84 us (level)
  no operation moved by 1% of the time
where the time goes in v5:
time: 84 us; the launch traced here: 83.8 us
  Pallas kernels  81.8 us (97%)
  local copies, waits for them, and re-layouts  1.41 us (2%)
    pallas_call x1, Pallas kernels, on_device(): pl.pallas_call(kernel, name='update_and_decode', out_shape=(pltpu.VMEM((6...  81.8 us

profile of v5, /device:TPU:1, one launch (start us, length us, event | category | flops | bytes accessed | tf_op | source)
XLA Modules:
  0.0 83.8 jit_solution(12569739010482810825)
XLA Ops:
  0.6 81.8 %update_and_decode.1 = (f32[64,1024]{1,0:T(8,128)S(1)}, bf16[4,32,1024]{2,1,0:T(8,128)(2,1)S(1)}) custom-call(s32[4,32]{1,0:T(4,128)} %bitcast.15, bf16[512,8192]{1,0:T(8,128)(2,1)} %acts.1, bf16[512,1024]{1,0:T(8,128)(2,1)} %cot.1, f32[64,1024]{1,0:T(8,128)} %master.1, f32[64,1024]{1,0:T(8,128)} %mom1.1, f32[64,1024]{1,0:T(8,128)} %mom2.1, ...), custom_call_target="tpu_custom_call" | custom-call | tf_op jit(solution)/shard_map/update_and_decode/pallas_call | solution.py:406
  82.4 0.7 copy.16
  83.1 0.7 copy.17
